TPU v7x, 256 devices: a whole 4x4x8 slice. The times are simulated.
256 devices in a mesh: section: 8 (over y_hi, x), ed: 32 (over y_lo, z, core).
Axes of the slice: x: 4, y: 4 (y_hi: 2, y_lo: 2; y = y_hi * 2 + y_lo), z: 8, core: 2. Of those that a mesh axis runs over, the one named last changes fastest.
Arguments:
- hidden: bfloat16 [512, 7168], P('ed'), may hold values from -24 to 24
- moe_gain: bfloat16 [7168], replicated, may hold values from 0.25 to 1.75
- expert_ids: int32 [512, 4], P('ed'), may hold values from 0 to 31, all different within a row; in each aligned block of 16 rows (0 to 15, 16 to 31, ...) at most 4 rows name the same one
- gate_weights: float32 [512, 4], P('ed'), may hold values from 0.1 to 1
- gate_matrix: bfloat16 [32, 7168, 1024], P('ed', None, 'section'), may hold values from -0.0625 to 0.0625
- up_matrix: bfloat16 [32, 7168, 1024], P('ed', None, 'section'), may hold values from -0.0625 to 0.0625
- down_matrix: bfloat16 [32, 1024, 7168], P('ed', 'section'), may hold values from -0.1875 to 0.1875
- head_gain: bfloat16 [7168], replicated, may hold values from 0.25 to 1.75
- head_table: bfloat16 [65536, 7168], P(('section', 'ed')), may hold values from -16 to 16
- targets: int32 [512], replicated, may hold values from 0 to 65535
- loss_weight: float32 [512], replicated, may hold values from 0.25 to 1
Outputs:
- block_out: bfloat16 [512, 7168], P('ed')
- loss: float32 [512], replicated
- head_grad: bfloat16 [65536, 7168], P(('section', 'ed'))
Inputs may be any that keep to these rules, and one draw needn't show every extreme that they name: `expert_ids`: each row names 4 different experts; the tokens of one index of ed name one expert 4 times at most.
All inputs are finite; a program needn't handle non-finite values.
Results may differ from a plain program's by a relative error of at most 0.015.
Values may be sent and summed in bfloat16 or wider, within the bound.
No kernel may reach another device: no remote copies, remote signals or barrier semaphores. Data moves between devices by JAX's collectives and lax.ppermute only.
A program may use at most 128 MiB of HBM per device.

v0:
```python
import jax
import jax.numpy as jnp
from jax import lax
from jax.sharding import PartitionSpec as P


def joined(value, axis, join):
    pieces = jax.tree.map(lambda part: lax.all_gather(part, axis), value)
    head = jax.tree.map(lambda part: part[0], pieces)
    tail = jax.tree.map(lambda part: part[1:], pieces)
    subtotal, _ = lax.scan(lambda subtotal, slab: (join(subtotal, slab), None), head, tail)
    return subtotal


def rms_scale(values, gain_vec, norm_axes):
    values = values.astype(jnp.float32)
    mean_square = jnp.mean(values * values, axis=norm_axes, keepdims=True)
    return values * lax.rsqrt(mean_square + 1e-06) * gain_vec.astype(jnp.float32)


def combine_stats(first_stats, second_stats):
    row_max = jnp.maximum(first_stats[0], second_stats[0])
    row_total = first_stats[1] * jnp.exp(first_stats[0] - row_max) + second_stats[1] * jnp.exp(
        second_stats[0] - row_max
    )
    return (row_max, row_total, first_stats[2] + second_stats[2])


def local(
    hidden,
    moe_gain,
    expert_ids,
    gate_weights,
    gate_matrix,
    up_matrix,
    down_matrix,
    head_gain,
    head_table,
    targets,
    loss_weight,
):
    tok_rows, model_width = hidden.shape
    groups = lax.axis_size("ed")
    top_count = expert_ids.shape[1]
    capacity = max(2, 2 * tok_rows * top_count // groups)
    normed = rms_scale(hidden, moe_gain, -1).astype(jnp.bfloat16)
    flat_ids = expert_ids.reshape(-1)
    expert_hot = (flat_ids[:, None] == jnp.arange(groups, dtype=jnp.int32)[None, :]).astype(
        jnp.int32
    )
    before = jnp.cumsum(expert_hot, axis=0) - expert_hot
    position = jnp.sum(before * expert_hot, axis=1)
    slot_of = (flat_ids * capacity + position).reshape(tok_rows, top_count)
    all_slots = jnp.arange(groups * capacity, dtype=jnp.int32)
    slot_hits = slot_of[:, :, None] == all_slots[None, None, :]
    place_map = jnp.any(slot_hits, axis=1).astype(jnp.bfloat16)
    blend_map = jnp.sum(jnp.where(slot_hits, gate_weights[:, :, None], 0.0), axis=1)
    outgoing = lax.dot_general(
        place_map, normed, (((0,), (0,)), ((), ())), preferred_element_type=jnp.float32
    )
    outgoing = outgoing.astype(jnp.bfloat16).reshape(groups, capacity, model_width)
    gate_local = gate_matrix[0]
    up_local = up_matrix[0]
    down_local = down_matrix[0]
    arrived = lax.all_to_all(outgoing, "ed", split_axis=0, concat_axis=0, tiled=True)
    gate_proj = jnp.einsum("gnd,dh->gnh", arrived, gate_local, preferred_element_type=jnp.float32)
    up_proj = jnp.einsum("gnd,dh->gnh", arrived, up_local, preferred_element_type=jnp.float32)
    inner_act = (jax.nn.silu(gate_proj) * up_proj).astype(jnp.bfloat16)
    expert_out = jnp.einsum(
        "gnh,hd->gnd", inner_act, down_local, preferred_element_type=jnp.float32
    )
    returned = lax.all_to_all(
        expert_out.astype(jnp.bfloat16), "ed", split_axis=0, concat_axis=0, tiled=True
    )
    returned_rows = returned.reshape(groups * capacity, -1).astype(jnp.float32)
    routed_part = jnp.dot(
        blend_map,
        returned_rows,
        precision=lax.Precision.HIGHEST,
        preferred_element_type=jnp.float32,
    )
    routed = lax.psum(routed_part.astype(jnp.bfloat16), "section").astype(jnp.float32)
    block_out = (hidden.astype(jnp.float32) + routed).astype(jnp.bfloat16)
    head_in = rms_scale(block_out, head_gain, -1).astype(jnp.bfloat16)
    gathered = lax.all_gather(head_in, "ed", axis=0, tiled=True)
    logits = lax.dot_general(
        gathered, head_table, (((1,), (1,)), ((), ())), preferred_element_type=jnp.float32
    )
    vocab_rows = head_table.shape[0]
    vocab_start = lax.axis_index(("section", "ed")) * vocab_rows
    vocab_ids = vocab_start + jnp.arange(vocab_rows, dtype=jnp.int32)
    is_target = vocab_ids[None, :] == targets[:, None]
    row_max = jnp.max(logits, axis=1)
    row_total = jnp.sum(jnp.exp(logits - row_max[:, None]), axis=1)
    target_logit = jnp.sum(jnp.where(is_target, logits, 0.0), axis=1)
    row_max, row_total, target_logit = joined(
        (row_max, row_total, target_logit), ("section", "ed"), combine_stats
    )
    spread = row_max + jnp.log(row_total)
    loss_all = spread - target_logit
    token_prob = jnp.exp(logits - spread[:, None])
    logit_grad = (loss_weight[:, None] * (token_prob - is_target.astype(jnp.float32))).astype(
        jnp.bfloat16
    )
    head_grad = lax.dot_general(
        logit_grad, gathered, (((0,), (0,)), ((), ())), preferred_element_type=jnp.float32
    )
    return (block_out, loss_all, head_grad.astype(jnp.bfloat16))


def solution(mesh):
    placed = (
        P("ed", None),
        P(),
        P("ed", None),
        P("ed", None),
        P("ed", None, "section"),
        P("ed", None, "section"),
        P("ed", "section", None),
        P(),
        P(("section", "ed"), None),
        P(),
        P(),
    )
    return jax.shard_map(
        local,
        mesh=mesh,
        in_specs=placed,
        out_specs=(P("ed", None), P(), P(("section", "ed"), None)),
        check_vma=False,
    )
```

profile of v0, /device:TPU:1, one launch (start us, length us, event | category | flops | bytes accessed | tf_op | source)
XLA Modules:
  0.0 1375.8 jit_solution(13840773103190202033)
XLA Ops:
  7.2 0.0 copy-start
  7.2 0.9 copy.35
  8.1 0.1 eq.20
  8.2 0.1 fusion.47
  8.2 0.1 reduce_window_sum.11
  8.3 0.2 select_reduce_fusion.1
  8.5 0.1 reduce_sum.57
  8.6 0.1 copy.36
  8.7 0.7 multiply_add_fusion.1
  9.4 0.1 fusion.46
  9.5 0.7 convert_element_type.53
  10.2 1.1 fusion.28
  11.3 2.9 convolution_convert_fusion.2
  14.2 4.1 reshape.47
  18.3 54.9 %all_to_all.10 = bf16[32,4,7168]{2,1,0:T(4,128)(2,1)S(1)} all-to-all(bf16[32,4,7168]{2,1,0:T(4,128)(2,1)} %reshape.47), channel_id=1, replica_groups=mesh['section'=8,'ed'=32] {'ed'}, dimensions={0} | all-to-all | bytes 3670016 | tf_op jit(solution)/shard_map/all_to_all | solution.py:65
  73.2 1.2 copy-done.1
  74.5 0.9 fusion.3
  75.3 4.9 convolution_convert_fusion.1
  80.2 4.1 copy.39
  84.3 6.8 all-to-all-start.1
  91.2 0.0 all-reduce.2.cloned.1.call-start
  91.2 0.0 copy-done.8
  91.2 0.1 select_reduce_fusion
  91.3 43.8 %all-to-all-done.1 = bf16[32,4,7168]{2,1,0:T(4,128)(2,1)} async-done(((bf16[32,4,7168]{2,1,0:T(4,128)(2,1)}), bf16[32,4,7168]{2,1,0:T(4,128)(2,1)}, u32[]{:S(2)}, u32[]{:S(2)}) %all-to-all-start.1) | async-done | bytes 1835040 | tf_op jit(solution)/shard_map/all_to_all | solution.py:72
  135.1 3.9 reshape.48
  139.0 3.1 convolution_convert_fusion.3
  142.1 0.0 all-reduce.2.cloned.1.call-update
  142.1 0.0 all-gather.8.cloned.1.call-start
  142.2 80.5 %all-reduce.2.cloned.1.call-done = bf16[16,7168]{1,0:T(8,128)(2,1)} async-done(((bf16[16,7168]{1,0:T(8,128)(2,1)}), bf16[16,7168]{1,0:T(8,128)(2,1)}) %all-reduce.2.cloned.1.call-update) | async-done | bytes 229392 | tf_op jit(solution)/shard_map/psum | solution.py:82
  222.7 1.1 fusion.25
  223.9 0.8 fusion.27
  224.7 0.0 all-gather.8.cloned.1.call-update
  224.7 0.0 copy-start.7
  224.8 77.8 %all-gather.8.cloned.1.call-done = bf16[512,7168]{1,0:T(8,128)(2,1)} async-done(((bf16[16,7168]{1,0:T(8,128)(2,1)}), bf16[512,7168]{1,0:T(8,128)(2,1)}) %all-gather.8.cloned.1.call-update) | async-done | bytes 7340048 | tf_op jit(solution)/shard_map/all_gather | solution.py:85
  302.6 6.2 fusion.51
  308.8 345.7 %all-gather.3 = f32[256,1,512]{2,1,0:T(1,128)S(1)} all-gather(f32[1,1,512]{2,1,0:T(1,128)S(1)} %bitcast.57), channel_id=2, replica_groups=mesh['section'=8,'ed'=32] {'section','ed'}, dimensions={0}, use_global_device_ids=true | all-gather | bytes 526336 | tf_op jit(solution)/shard_map/all_gather | solution.py:8
  654.5 0.4 slice.39
  654.9 0.1 fusion.21
  655.0 340.5 %all-gather.4 = f32[256,1,512]{2,1,0:T(1,128)S(1)} all-gather(f32[1,1,512]{2,1,0:T(1,128)S(1)} %bitcast.59), channel_id=3, replica_groups=mesh['section'=8,'ed'=32] {'section','ed'}, dimensions={0}, use_global_device_ids=true | all-gather | bytes 526336 | tf_op jit(solution)/shard_map/all_gather | solution.py:8
  995.6 0.4 slice.40
  995.9 341.9 %all-gather.5 = f32[256,1,512]{2,1,0:T(1,128)S(1)} all-gather(f32[1,1,512]{2,1,0:T(1,128)S(1)} %bitcast.58), channel_id=4, replica_groups=mesh['section'=8,'ed'=32] {'section','ed'}, dimensions={0}, use_global_device_ids=true | all-gather | bytes 526336 | tf_op jit(solution)/shard_map/all_gather | solution.py:8
  1337.8 0.4 slice.41
  1338.2 0.0 slice-start
  1338.2 0.0 copy-start.10
  1338.3 0.5 slice-done
  1338.8 22.2 %while.14 = (s32[]{:T(128)}, f32[512]{0:T(512)S(1)}, f32[512]{0:T(512)S(1)}, f32[512]{0:T(512)S(1)}, f32[255,512]{1,0:T(8,128)S(1)}, /*index=5*/f32[255,512]{1,0:T(8,128)S(1)}, f32[255,512]{1,0:T(8,128)S(1)}, s32[]{:T(128)}) while((s32[]{:T(128)}, f32[512]{0:T(512)S(1)}, f32[512]{0:T(512)S(1)}, f32[512]{0:T(512)S(1)}, ...), condition=%wide.region_11.12_spmd, body=%wide.region_10.11_spmd.sunk | while | flops 3586 | bytes 30821 | solution.py:11
  1361.1 0.6 fusion.49
  1361.7 7.3 convolution_convert_fusion
  (1046 shorter events, 13.8 us)
Async XLA Ops:
  7.2 68.2 %copy-start = (bf16[1,128,7168]{2,1,0:T(8,128)(2,1)S(1)}, bf16[1,128,7168]{2,1,0:T(8,128)(2,1)}, u32[]{:S(2)}) copy-start(bf16[1,128,7168]{2,1,0:T(8,128)(2,1)} %param.19) | copy-start | bytes 5505028
  18.3 56.2 %copy-start.9 = (bf16[1,7168,128]{2,1,0:T(8,128)(2,1)S(1)}, bf16[1,7168,128]{2,1,0:T(8,128)(2,1)}, u32[]{:S(2)}) copy-start(bf16[1,7168,128]{2,1,0:T(8,128)(2,1)} %param.17) | copy-start | bytes 5505028
  73.2 1.2 copy-start.1
  84.3 6.9 copy-start.8
  84.3 50.8 %all-to-all-start.1 = ((bf16[32,4,7168]{2,1,0:T(4,128)(2,1)}), bf16[32,4,7168]{2,1,0:T(4,128)(2,1)}, u32[]{:S(2)}, u32[]{:S(2)}) async-start(bf16[32,4,7168]{2,1,0:T(4,128)(2,1)} %copy.39), calls=%async_computation.1 | async-start | bytes 3670016 | tf_op jit(solution)/shard_map/all_to_all | solution.py:72
  91.2 131.5 %all-reduce.2.cloned.1.call-start = ((), (), s32[]{:S(2)}) async-start(), calls=%async_computation.2 | async-start | bytes 458752 | tf_op jit(solution)/shard_map/psum | solution.py:82
  139.0 3.1 copy-start.6
  139.0 83.7 %copy-start.3 = (bf16[16,7168]{1,0:T(8,128)(2,1)S(1)}, bf16[16,7168]{1,0:T(8,128)(2,1)}, u32[]{:S(2)}) copy-start(bf16[16,7168]{1,0:T(8,128)(2,1)} %param.13) | copy-start | bytes 688132
  142.1 160.4 %all-gather.8.cloned.1.call-start = ((), (), s32[]{:S(2)}) async-start(), calls=%async_computation.3 | async-start | bytes 7569408 | tf_op jit(solution)/shard_map/all_gather | solution.py:85
  223.9 84.9 %copy-start.4 = (bf16[16,7168]{1,0:T(8,128)(2,1)}, bf16[16,7168]{1,0:T(8,128)(2,1)S(1)}, u32[]{:S(2)}) copy-start(bf16[16,7168]{1,0:T(8,128)(2,1)S(1)} %get-tuple-element.66) | copy-start | bytes 688132
  224.7 430.1 %copy-start.7 = (s32[512]{0:T(512)S(1)}, s32[512]{0:T(512)}, u32[]{:S(2)}) copy-start(s32[512]{0:T(512)} %param.22) | copy-start | bytes 6148
  308.8 687.1 %copy-start.5 = (f32[512,256]{0,1:T(8,128)}, f32[512,256]{0,1:T(8,128)S(1)}, u32[]{:S(2)}) copy-start(f32[512,256]{0,1:T(8,128)S(1)} %get-tuple-element.70) | copy-start | bytes 1572868
  654.5 683.3 %copy-start.2 = (f32[256,1,512]{2,1,0:T(1,128)}, f32[256,1,512]{2,1,0:T(1,128)S(1)}, u32[]{:S(2)}) copy-start(f32[256,1,512]{2,1,0:T(1,128)S(1)} %all-gather.3) | copy-start | bytes 1572868
  1338.2 0.7 slice-start
  1338.2 23.5 %copy-start.10 = (f32[512]{0:T(512)S(1)}, f32[512]{0:T(512)}, u32[]{:S(2)}) copy-start(f32[512]{0:T(512)} %param.23) | copy-start | bytes 6148
Sparse Core Ops, SparseCore 0:
  142.2 80.4 all-reduce.1
  225.3 77.2 all-gather.7
where the time goes:
time: 1380 us
  blocking collectives  1080 us (78%)
  waiting for transfers between devices  202 us (15%)
  matrix products  25.1 us (2%)
  local copies, waits for them, and re-layouts  22.5 us (2%)
  between operations  14.3 us (1%)
    all_gather x3, blocking collectives, joined(): pieces = jax.tree.map(lambda part: lax.all_gather(part, axis), value)  1030 us
    psum x1, waiting for transfers between devices, local(): lax.psum(routed_part.astype(jnp.bfloat16), 'section').astype(jnp.float32)  80.5 us
    all_gather x1, waiting for transfers between devices, local(): gathered = lax.all_gather(head_in, 'ed', axis=0, tiled=True)  77.8 us
    all_to_all x1, blocking collectives, local(): lax.all_to_all(outgoing, 'ed', split_axis=0, concat_axis=0, tiled=True)  54.9 us
    all_to_all x1, waiting for transfers between devices, local(): lax.all_to_all(expert_out.astype(jnp.bfloat16), 'ed', split_axis=0, conca...  43.8 us
  transfers between devices with their start and end apart: 3, of which 3 were waited for; matrix products, arithmetic and copies ran while one was open for 0% of the time, Pallas kernels for 0%

commit v1 on v0

v1 whole, which is shorter than its diff:
```python
import jax
import jax.numpy as jnp
from jax import lax
from jax.experimental import pallas as pl
from jax.experimental.pallas import tpu as pltpu
from jax.sharding import Mesh
from jax.sharding import PartitionSpec as P

AXES = ("y_hi", "x", "y_lo", "z", "core")
SIZES = (2, 4, 2, 8, 2)
SECTION = ("y_hi", "x")
ED = ("y_lo", "z", "core")
CHIP = ("y_lo", "z")
SECTION_CORE = SECTION + ("core",)
TOP = 4
CAP = 4
ROWS = 16
N_ED = 32
N_SEC = 8
N_X = 4
LANES = 128
PARTS = 2
OUT_PARTS = 4
F32 = jnp.float32
BF16 = jnp.bfloat16
VMEM_LIMIT = 58 * 1024 * 1024


def pairs_of(move):
    pairs = []
    y_hi_n, x_n, y_lo_n, z_n, core_n = SIZES
    for y_hi in range(y_hi_n):
        for x in range(x_n):
            for y_lo in range(y_lo_n):
                for z in range(z_n):
                    for core in range(core_n):
                        y, x2, z2, core2 = move(y_hi * y_lo_n + y_lo, x, z, core)
                        y, x2, z2 = y % (y_hi_n * y_lo_n), x2 % x_n, z2 % z_n
                        here = (((y_hi * x_n + x) * y_lo_n + y_lo) * z_n + z) * core_n + core
                        there = (
                            ((y // y_lo_n * x_n + x2) * y_lo_n + y % y_lo_n) * z_n + z2
                        ) * core_n + core2
                        pairs.append((here, there))
    return pairs


FROM_Z = pairs_of(lambda y, x, z, c: (y, x, z - 1 + 2 * c, c))
FROM_Y = pairs_of(lambda y, x, z, c: (y - 1 + 2 * c, x, z, c))
FROM_CORE = pairs_of(lambda y, x, z, c: (y, x, z, 1 - c))
FROM_Y_HI = pairs_of(lambda y, x, z, c: (y + 2, x, z, c))
FROM_X = [pairs_of(lambda y, x, z, c, d=d: (y, x - d, z, c)) for d in range(N_X)]


def take(value, pairs):
    return lax.ppermute(value, AXES, pairs)


RING = [(k, y, 2 * ROWS if 0 < k < 4 else ROWS) for y in (0, 1) for k in (0, 1, 2, 3, 4)]
PLACES = [(0, 0, 0, 2 * ROWS)]
PLACES += [(k, y, swap, n) for swap in (0, 1) for k, y, n in RING if (k, y) != (0, 0)]
N_PIECES = len(PLACES)


def own_rows(block):
    return lax.dynamic_slice_in_dim(block, lax.axis_index("core") * ROWS, ROWS, axis=0)


def gather_ed(block, own):
    z1 = take(block, FROM_Z)
    y0 = take(own, FROM_Y)
    z2 = take(z1, FROM_Z)
    y1 = take(z1, FROM_Y)
    z3 = take(z2, FROM_Z)
    y2 = take(z2, FROM_Y)
    z4 = take(own_rows(z3), FROM_Z)
    y3 = take(z3, FROM_Y)
    y4 = take(z4, FROM_Y)
    ring = [z1, z2, z3, z4, y0, y1, y2, y3, y4]
    return [block] + ring + [take(piece, FROM_CORE) for piece in ring]


CHUNKS = [(0, 0), (0, 1), (1, 0), (3, 0), (2, 0), (1, 1), (3, 1), (2, 1)]


def gather_section(part):
    got = {(0, 0): part, (0, 1): take(part, FROM_Y_HI)}
    for d in (1, 3, 2):
        got[d, 0] = take(part, FROM_X[d])
    got[2, 1] = take(got[2, 0], FROM_Y_HI)
    for d in (1, 3):
        got[d, 1] = take(got[0, 1], FROM_X[d])
    return [got[chunk] for chunk in CHUNKS]


def chunk_start(chunk, steps=0, other=0):
    x, y_hi = lax.axis_index("x"), lax.axis_index("y_hi")
    from_y = 1 - y_hi if other else y_hi
    return ((x + steps) % N_X * 2 + from_y) * chunk


def column_cuts(width):
    part = width // (PARTS * LANES) * LANES
    first = width - part * (PARTS - 1)
    return [(0, first)] + [(first + p * part, part) for p in range(PARTS - 1)]


def start_rows(pieces, rows_ref, sems):
    core, z, y_lo = lax.axis_index("core"), lax.axis_index("z"), lax.axis_index("y_lo")
    all_copies = []
    for p, (at, size) in enumerate(column_cuts(rows_ref.shape[1])):
        copies = []
        for k, (step, other_y, swap, n) in enumerate(PLACES):
            ring = 1 - core if swap else core
            from_z = (z + step + 8 * ring - 2 * step * ring) % 8
            from_y = 1 - y_lo if other_y else y_lo
            start = (from_y * 8 + from_z) * 2 * ROWS
            if n == ROWS:
                start = start + ring * ROWS
            copy = pltpu.make_async_copy(
                pieces[k].at[:, pl.ds(at, size)],
                rows_ref.at[pl.ds(pl.multiple_of(start, ROWS), n), pl.ds(at, size)],
                sems.at[p, k],
            )
            copy.start()
            copies.append(copy)
        all_copies.append(copies)
    return all_copies


def dot(a, b, dims=((1,), (0,))):
    return lax.dot_general(a, b, (dims, ((), ())), preferred_element_type=F32)


def expert_index():
    return (lax.axis_index("y_lo") * 8 + lax.axis_index("z")) * 2 + lax.axis_index("core")


def dispatch_kernel(hidden, ids, weights, gain, down, slots, blend, *refs):
    quarters, (normed, sems) = refs[:N_X], refs[N_X:]
    width = hidden.shape[1]
    quarter, chunk = width // N_X, width // N_SEC
    x = lax.axis_index("x")
    copies = []
    for d in range(N_X):
        start = pl.multiple_of((x + N_X - d) % N_X * quarter, LANES)
        copy = pltpu.make_async_copy(
            down.at[:, pl.ds(start, quarter)], quarters[d], sems.at[d]
        )
        copy.start()
        copies.append(copy)
    value = hidden[...].astype(F32)
    scale = lax.rsqrt(jnp.mean(value * value, axis=-1, keepdims=True) + 1e-06)
    normed[...] = (value * scale * gain[...].astype(F32).reshape(1, width)).astype(BF16)
    slot = lax.broadcasted_iota(jnp.int32, (N_ED * CAP, ROWS), 0)
    hit = jnp.zeros((N_ED * CAP, ROWS), F32)
    weight = jnp.zeros((N_ED * CAP, ROWS), F32)
    for k in range(TOP):
        named = ids[k : k + 1, :] == slot // CAP
        hit = jnp.where(named, 1.0, hit)
        weight = jnp.where(named, weights[k : k + 1, :], weight)
    row_of = lax.broadcasted_iota(jnp.int32, (ROWS, ROWS), 0)
    col_of = lax.broadcasted_iota(jnp.int32, (ROWS, ROWS), 1)
    before = dot(hit.astype(BF16), jnp.where(row_of < col_of, 1.0, 0.0).astype(BF16))
    placed = (hit > 0.0) & (before == (slot % CAP).astype(F32))
    blend[...] = jnp.where(placed, weight, 0.0)
    own = normed[:, pl.ds(pl.multiple_of(chunk_start(chunk), LANES), chunk)]
    slots[...] = dot(jnp.where(placed, 1.0, 0.0).astype(BF16), own).astype(BF16)
    for copy in copies:
        copy.wait()


def run_dispatch(hidden, ids, weights, gain, down):
    rows, width = hidden.shape
    quarter = jax.ShapeDtypeStruct((down.shape[0], width // N_X), BF16)
    vmem = pl.BlockSpec(memory_space=pltpu.VMEM)
    hbm = pl.BlockSpec(memory_space=pltpu.HBM)
    outs = pl.pallas_call(
        dispatch_kernel,
        out_shape=[
            jax.ShapeDtypeStruct((N_ED * CAP, width // N_SEC), BF16),
            jax.ShapeDtypeStruct((N_ED * CAP, rows), F32),
        ]
        + [quarter] * N_X,
        in_specs=[vmem] * 4 + [hbm],
        out_specs=[vmem] * (2 + N_X),
        scratch_shapes=[pltpu.VMEM((rows, width), BF16), pltpu.SemaphoreType.DMA((N_X,))],
        compiler_params=pltpu.CompilerParams(vmem_limit_bytes=16 * 1024 * 1024),
        name="dispatch",
    )(hidden, ids, weights, gain, down)
    return outs[0], outs[1], outs[2:]


def row_shapes(width):
    return [jax.ShapeDtypeStruct((n * ROWS, width), BF16) for n in (2, 1)]


def run_pack(own, other, own_names, other_names, gain):
    vmem = pl.BlockSpec(memory_space=pltpu.VMEM)
    return pl.pallas_call(
        pack_kernel,
        out_shape=row_shapes(own.shape[1] + LANES),
        in_specs=[vmem] * 5,
        out_specs=[vmem] * 2,
        name="pack",
    )(own, other, own_names, other_names, gain)


def head_kernel(chunks, gain, block_out, block, alone):
    core = lax.axis_index("core")
    chunk = chunks.shape[2]
    width = N_SEC * chunk
    gains = gain[...].astype(F32).reshape(1, width)
    for k in range(2):
        of_core = core if k == 0 else 1 - core
        rows = pl.ds(pl.multiple_of(of_core * ROWS, ROWS), ROWS)
        square = jnp.zeros((ROWS, 1), F32)
        for s in range(N_SEC):
            value = chunks[2 * s + of_core].astype(F32)
            square = square + jnp.sum(value * value, axis=-1, keepdims=True)
        scale = lax.rsqrt(square / width + 1e-06)
        for s in range(N_SEC):
            at = (s % N_X * 2 + s // N_X) * chunk
            cut = slice(at, at + chunk)
            own = chunks[2 * s + of_core]
            normed = (own.astype(F32) * scale * gains[:, cut]).astype(BF16)
            block[rows, cut] = normed
            if k == 0:
                alone[:, cut] = normed
                block_out[:, cut] = own


def run_head(chunks, gain):
    width = N_SEC * chunks.shape[2]
    vmem = pl.BlockSpec(memory_space=pltpu.VMEM)
    return pl.pallas_call(
        head_kernel,
        out_shape=[jax.ShapeDtypeStruct((ROWS, width), BF16)] + row_shapes(width),
        in_specs=[vmem] * 2,
        out_specs=[vmem] * 3,
        name="head_norm",
    )(chunks, gain)


def inner_kernel(*refs):
    pieces, (gate, up, out, gate_up, sems) = refs[:N_SEC], refs[N_SEC:]
    chunk = pieces[0].shape[1]
    copies = []
    for k, (steps, other) in enumerate(CHUNKS):
        rows = pl.ds(pl.multiple_of(chunk_start(chunk, steps, other), LANES), chunk)
        for j, weight in enumerate((gate, up)):
            copy = pltpu.make_async_copy(
                weight.at[rows, :], gate_up.at[k, :, pl.ds(j * LANES, LANES)], sems.at[2 * k + j]
            )
            copy.start()
            copies.append(copy)
    total = None
    for k in range(N_SEC):
        copies[2 * k].wait()
        copies[2 * k + 1].wait()
        product = dot(pieces[k][...], gate_up[k])
        total = product if total is None else total + product
    gate_proj, up_proj = total[:, :LANES], total[:, LANES:]
    out[...] = (gate_proj / (1.0 + jnp.exp(-gate_proj)) * up_proj).astype(BF16)


def run_inner(pieces, gate, up):
    vmem = pl.BlockSpec(memory_space=pltpu.VMEM)
    hbm = pl.BlockSpec(memory_space=pltpu.HBM)
    slots, chunk = pieces[0].shape
    return pl.pallas_call(
        inner_kernel,
        out_shape=jax.ShapeDtypeStruct((slots, LANES), BF16),
        in_specs=[vmem] * N_SEC + [hbm] * 2,
        out_specs=vmem,
        scratch_shapes=[
            pltpu.VMEM((N_SEC, chunk, 2 * LANES), BF16),
            pltpu.SemaphoreType.DMA((2 * N_SEC,)),
        ],
        compiler_params=pltpu.CompilerParams(vmem_limit_bytes=VMEM_LIMIT),
        name="inner",
    )(*pieces, gate, up)


def down_kernel(*refs):
    inner, down, (keep, send, total) = refs[:N_X], refs[N_X : 2 * N_X], refs[2 * N_X :]
    acc = dot(inner[0][...], down[0][...])
    for d in range(1, N_X):
        acc = acc + dot(inner[d][...], down[d][...])
    total[...] = acc
    chunk = keep.shape[1]
    y_hi = lax.axis_index("y_hi")
    keep[...] = total[:, pl.ds(pl.multiple_of(y_hi * chunk, LANES), chunk)]
    send[...] = total[:, pl.ds(pl.multiple_of((1 - y_hi) * chunk, LANES), chunk)].astype(BF16)


def run_down(inner, down):
    slots, quarter = inner[0].shape[0], down[0].shape[1]
    vmem = pl.BlockSpec(memory_space=pltpu.VMEM)
    return pl.pallas_call(
        down_kernel,
        out_shape=(
            jax.ShapeDtypeStruct((slots, quarter // 2), F32),
            jax.ShapeDtypeStruct((slots, quarter // 2), BF16),
        ),
        in_specs=[vmem] * (2 * N_X),
        out_specs=(vmem, vmem),
        scratch_shapes=[pltpu.VMEM((slots, quarter), F32)],
        compiler_params=pltpu.CompilerParams(vmem_limit_bytes=VMEM_LIMIT),
        name="down",
    )(*inner, *down)


def vocab_start(vocab):
    section = lax.axis_index("y_hi") * N_X + lax.axis_index("x")
    return (section * N_ED + expert_index()) * vocab


def logits_kernel(*refs):
    pieces, (table, targets, logits, stats, gathered, rows, table_v, sems, table_sems) = (
        refs[:N_PIECES],
        refs[N_PIECES:],
    )
    vocab, tokens = logits.shape
    part = table.shape[1] // PARTS
    table_copies = []
    for p in range(PARTS):
        cut = pl.ds(p * part, part)
        copy = pltpu.make_async_copy(table.at[:, cut], table_v.at[:, cut], table_sems.at[p])
        copy.start()
        table_copies.append(copy)
    copies = start_rows(pieces, rows, sems)
    out_copies = []
    for p in range(PARTS):
        for copy in [table_copies[p]] + copies[p]:
            copy.wait()
        out_cut = pl.ds(p * part, part)
        out_copies.append(
            pltpu.make_async_copy(
                rows.at[:, out_cut], gathered.at[:, out_cut], table_sems.at[PARTS + p]
            )
        )
        out_copies[p].start()
        cut = slice(p * part, (p + 1) * part)
        product = dot(table_v[:, cut], rows[:, cut], ((1,), (1,)))
        if p == 0:
            logits[...] = product
        else:
            logits[...] += product
    first = vocab_start(vocab)
    lines = tokens // LANES
    found = [[], [], []]
    for k in range(lines):
        cut = slice(k * LANES, (k + 1) * LANES)
        value = logits[:, cut]
        vocab_ids = first + lax.broadcasted_iota(jnp.int32, value.shape, 0)
        row_max = jnp.max(value, axis=0, keepdims=True)
        hot = vocab_ids == targets[:, cut]
        found[0].append(row_max)
        found[1].append(jnp.sum(jnp.exp(value - row_max), axis=0, keepdims=True))
        found[2].append(jnp.sum(jnp.where(hot, value, 0.0), axis=0, keepdims=True))
    spread_out([jnp.concatenate(values, axis=0) for values in found], stats)
    for copy in out_copies:
        copy.wait()


def run_logits(pieces, table, targets):
    vocab, width = table.shape
    tokens = N_ED * ROWS
    lines = tokens // LANES
    vmem = pl.BlockSpec(memory_space=pltpu.VMEM)
    hbm = pl.BlockSpec(memory_space=pltpu.HBM)
    return pl.pallas_call(
        logits_kernel,
        out_shape=(
            jax.ShapeDtypeStruct((vocab, tokens), F32),
            jax.ShapeDtypeStruct((2 * N_SEC, 3 * lines, LANES), F32),
            jax.ShapeDtypeStruct((tokens, width), BF16),
        ),
        in_specs=[pl.BlockSpec(memory_space=pl.ANY)] * N_PIECES + [hbm, vmem],
        out_specs=(vmem, vmem, hbm),
        scratch_shapes=[
            pltpu.VMEM((tokens, width), BF16),
            pltpu.VMEM((vocab, width), BF16),
            pltpu.SemaphoreType.DMA((PARTS, N_PIECES)),
            pltpu.SemaphoreType.DMA((2 * PARTS,)),
        ],
        compiler_params=pltpu.CompilerParams(vmem_limit_bytes=VMEM_LIMIT),
        name="logits",
    )(*pieces, table, targets)


def join_stats(parts):
    lines = parts.shape[1] // 3
    maxima = parts[:, 0:lines]
    row_max = jnp.max(maxima, axis=0)
    total = jnp.sum(parts[:, lines : 2 * lines] * jnp.exp(maxima - row_max[None]), axis=0)
    return row_max, total, jnp.sum(parts[:, 2 * lines :], axis=0)


def spread_out(stats, out):
    row_max, total, target = stats
    lines = row_max.shape[0]
    for k in range(out.shape[0]):
        out[k, 0:lines] = row_max
        out[k, lines : 2 * lines] = total
        out[k, 2 * lines : 3 * lines] = target


def join_kernel(parts, out):
    spread_out(join_stats(parts[...]), out)


def run_join(kernel, operands, shape):
    vmem = pl.BlockSpec(memory_space=pltpu.VMEM)
    return pl.pallas_call(
        kernel,
        out_shape=jax.ShapeDtypeStruct(shape, F32),
        in_specs=[vmem] * len(operands),
        out_specs=vmem,
        name="join",
    )(*operands)


def grad_kernel(gathered, parts, logits, targets, weight, loss, grad, rows, grad_v, sems):
    vocab, tokens = logits.shape
    part = rows.shape[1] // OUT_PARTS
    in_copies = []
    for p in range(OUT_PARTS):
        cut = pl.ds(p * part, part)
        copy = pltpu.make_async_copy(gathered.at[:, cut], rows.at[:, cut], sems.at[p])
        copy.start()
        in_copies.append(copy)
    first = vocab_start(vocab)
    row_max, total, target = join_stats(parts[...])
    spread = row_max + jnp.log(total)
    loss[...] = spread - target
    lines = []
    for k in range(tokens // LANES):
        cut = slice(k * LANES, (k + 1) * LANES)
        vocab_ids = first + lax.broadcasted_iota(jnp.int32, (vocab, LANES), 0)
        prob = jnp.exp(logits[:, cut] - spread[k : k + 1, :])
        hot = jnp.where(vocab_ids == targets[:, cut], 1.0, 0.0)
        lines.append((weight[:, cut] * (prob - hot)).astype(BF16))
    logit_grad = jnp.concatenate(lines, axis=1)
    out_copies = []
    for p in range(OUT_PARTS):
        in_copies[p].wait()
        cut = slice(p * part, (p + 1) * part)
        grad_v[p] = dot(logit_grad, rows[:, cut]).astype(BF16)
        copy = pltpu.make_async_copy(
            grad_v.at[p], grad.at[:, pl.ds(p * part, part)], sems.at[OUT_PARTS + p]
        )
        copy.start()
        out_copies.append(copy)
    for copy in out_copies:
        copy.wait()


def run_grad(gathered, parts, logits, targets, weight):
    (vocab, tokens), width = logits.shape, gathered.shape[1]
    vmem = pl.BlockSpec(memory_space=pltpu.VMEM)
    hbm = pl.BlockSpec(memory_space=pltpu.HBM)
    return pl.pallas_call(
        grad_kernel,
        out_shape=(
            jax.ShapeDtypeStruct((tokens // LANES, LANES), F32),
            jax.ShapeDtypeStruct((vocab, width), BF16),
        ),
        in_specs=[hbm] + [vmem] * 4,
        out_specs=(vmem, hbm),
        scratch_shapes=[
            pltpu.VMEM((tokens, width), BF16),
            pltpu.VMEM((OUT_PARTS, vocab, width // OUT_PARTS), BF16),
            pltpu.SemaphoreType.DMA((2 * OUT_PARTS,)),
        ],
        compiler_params=pltpu.CompilerParams(vmem_limit_bytes=VMEM_LIMIT),
        name="head_grad",
    )(gathered, parts, logits, targets, weight)


def local(
    hidden,
    moe_gain,
    expert_ids,
    gate_weights,
    gate_matrix,
    up_matrix,
    down_matrix,
    head_gain,
    head_table,
    targets,
    loss_weight,
):
    rows, width = hidden.shape
    chunk = width // N_SEC
    tokens = targets.shape[0]
    slots, blend, down = run_dispatch(
        hidden, expert_ids.T, gate_weights.T, moe_gain, down_matrix[0]
    )
    down = [take(part, FROM_X[d]) if d else part for d, part in enumerate(down)]
    arrived = lax.all_to_all(slots.reshape(N_ED, CAP, chunk), ED, 0, 0, tiled=True)
    arrived, down = lax.optimization_barrier((arrived, down))
    pieces = gather_section(arrived.reshape(N_ED * CAP, chunk))
    inner = run_inner(pieces, gate_matrix[0], up_matrix[0])
    inner = [take(inner, FROM_X[d]) if d else inner for d in range(N_X)]
    keep, send = run_down(inner, down)
    summed = (keep + take(send, FROM_Y_HI).astype(F32)).astype(BF16)
    returned = lax.all_to_all(summed.reshape(N_ED, CAP, chunk), ED, 0, 0, tiled=True)
    routed = lax.dot_general(
        blend,
        returned.reshape(N_ED * CAP, chunk).astype(F32),
        (((0,), (0,)), ((), ())),
        precision=lax.Precision.HIGHEST,
        preferred_element_type=F32,
    )
    own = lax.dynamic_slice_in_dim(hidden, chunk_start(chunk), chunk, axis=1)
    block_part = (own.astype(F32) + routed).astype(BF16)
    chunks = lax.all_to_all(
        jnp.broadcast_to(block_part[None], (2 * N_SEC, rows, chunk)),
        SECTION_CORE,
        0,
        0,
        tiled=True,
    )
    block_out, block, own = run_head(chunks, head_gain)
    pieces = gather_ed(block, own)
    targets_row, weight_row = targets.reshape(1, tokens), loss_weight.reshape(1, tokens)
    logits, stats, gathered = run_logits(pieces, head_table, targets_row)
    parts = lax.all_to_all(stats, SECTION_CORE, 0, 0, tiled=True)
    parts = run_join(join_kernel, (parts,), (N_ED // 2,) + stats.shape[1:])
    parts = lax.all_to_all(parts, CHIP, 0, 0, tiled=True)
    loss, head_grad = run_grad(gathered, parts, logits, targets_row, weight_row)
    return block_out, loss.reshape(tokens), head_grad


def solution(mesh):
    fine = Mesh(mesh.devices.reshape(SIZES), AXES)
    placed = (
        P(ED, None),
        P(),
        P(ED, None),
        P(ED, None),
        P(ED, None, SECTION),
        P(ED, None, SECTION),
        P(ED, SECTION, None),
        P(),
        P(SECTION + ED, None),
        P(),
        P(),
    )
    return jax.shard_map(
        local,
        mesh=fine,
        in_specs=placed,
        out_specs=(P(ED, None), P(), P(SECTION + ED, None)),
        check_vma=False,
    )
```

time: 1380 us -> 211 us (0.15)
  blocking collectives: 1080 us -> 62.8 us
  waiting for transfers between devices: 202 us -> 59.3 us
  starting transfers between devices: 6.93 us -> 47.5 us
  Pallas kernels: 0 us -> 28.3 us
  matrix products: 25.1 us -> 1.02 us
    all_gather x3 -> x0, blocking collectives: 1030 us -> none  [joined(): pieces = jax.tree.map(lambda part: lax.all_gather(part, axis), value)]
    psum x1 -> x0, waiting for transfers between devices: 80.5 us -> none  [local(): lax.psum(routed_part.astype(jnp.bfloat16), 'section').astype(jnp.float32)]
    all_gather x1 -> x0, waiting for transfers between devices: 77.8 us -> none  [local(): gathered = lax.all_gather(head_in, 'ed', axis=0, tiled=True)]
    ppermute x0 -> x32, waiting for transfers between devices: none -> 48.4 us  [take(): return lax.ppermute(value, AXES, pairs)]
    all_to_all x1, waiting for transfers between devices: 43.8 us -> 10.8 us  [local(): lax.all_to_all(summed.reshape(N_ED, CAP, chunk), ED, 0, 0, tiled=True)]
    ppermute x0 -> x32, starting transfers between devices: none -> 31.8 us  [take(): return lax.ppermute(value, AXES, pairs)]
    pallas_call x0 -> x7, Pallas kernels: none -> 28.3 us  [the longest x1 8.63 us: run_logits(): pl.pallas_call(logits_kernel, out_shape=(jax.ShapeDtypeStruct((vocab, tok...]
    dot_general x6 -> x1, matrix products: 25.1 us -> 1.02 us  [local(): lax.dot_general(blend, returned.reshape(N_ED * CAP, chunk).astype(F32), (...]
  transfers between devices with their start and end apart: 3 -> 33, of which waited for: 3 -> 17; matrix products, arithmetic and copies ran while one was open for 0% -> 0% of each run, Pallas kernels for 0% -> 0%
where the time goes in v1:
time: 211 us; the launch traced here: 210 us
  blocking collectives  62.8 us (30%)
  waiting for transfers between devices  59.3 us (28%)
  starting transfers between devices  47.5 us (23%)
  Pallas kernels  28.3 us (13%)
  local copies, waits for them, and re-layouts  8.99 us (4%)
    ppermute x32, waiting for transfers between devices, take(): return lax.ppermute(value, AXES, pairs)  48.4 us
    ppermute x32, starting transfers between devices, take(): return lax.ppermute(value, AXES, pairs)  31.8 us
    all_to_all x1, blocking collectives, local(): lax.all_to_all(slots.reshape(N_ED, CAP, chunk), ED, 0, 0, tiled=True)  21.8 us
    all_to_all x1, blocking collectives, local(): lax.all_to_all(jnp.broadcast_to(block_part[None], (2 * N_SEC, rows, chunk...  16.8 us
    all_to_all x1, starting transfers between devices, local(): lax.all_to_all(summed.reshape(N_ED, CAP, chunk), ED, 0, 0, tiled=True)  15.7 us
    all_to_all x1, blocking collectives, local(): parts = lax.all_to_all(parts, CHIP, 0, 0, tiled=True)  12.1 us
    all_to_all x1, blocking collectives, local(): parts = lax.all_to_all(stats, SECTION_CORE, 0, 0, tiled=True)  12 us
    all_to_all x1, waiting for transfers between devices, local(): lax.all_to_all(summed.reshape(N_ED, CAP, chunk), ED, 0, 0, tiled=True)  10.8 us
  transfers between devices with their start and end apart: 33, of which 17 were waited for; matrix products, arithmetic and copies ran while one was open for 0% of the time, Pallas kernels for 0%

profile of v1, /device:TPU:1, one launch (start us, length us, event | category | flops | bytes accessed | tf_op | source)
XLA Modules:
  0.0 210.2 jit_solution(9206098516148064643)
XLA Ops:
  0.6 1.5 copy-done
  2.1 0.9 copy-done.2
  3.1 0.7 copy-done.3
  3.8 0.7 copy-done.4
  4.5 0.7 copy-done.5
  5.8 0.8 copy-done.1
  6.6 3.3 %collective-permute-start = (bf16[128,1792]{1,0:T(8,128)(2,1)S(1)}, bf16[128,1792]{1,0:T(8,128)(2,1)S(1)}, u32[]{:S(2)}, u32[]{:S(2)}) collective-permute-start(bf16[128,1792]{1,0:T(8,128)(2,1)S(1)} %get-tuple-element.27), channel_id=1, source_target_pairs={{0,96},{1,97},{2,98},{3,99},{4,100},{5,101},{6,102},{7,103},{8,104... | collective-permute-start | bytes 1376264 | tf_op jit(solution)/shard_map/ppermute | solution.py:55
  11.1 21.8 %all_to_all.25 = bf16[32,4,896]{2,1,0:T(4,128)(2,1)S(1)} all-to-all(bf16[32,4,896]{2,1,0:T(4,128)(2,1)S(1)} %reshape.28), channel_id=1, replica_groups=mesh['y_hi'=2,'x'=4,'y_lo'=2,'z'=8,'core'=2] {'y_lo','z','core'}, dimensions={0} | all-to-all | bytes 458752 | tf_op jit(solution)/shard_map/all_to_all | solution.py:501
  32.9 0.8 collective-permute-done.2.refs_7_
  33.7 0.9 collective-permute-start.6
  34.7 2.6 %collective-permute-start.3 = (bf16[128,896]{1,0:T(8,128)(2,1)S(1)}, bf16[128,896]{1,0:T(8,128)(2,1)S(1)}, u32[]{:S(2)}, u32[]{:S(2)}) collective-permute-start(bf16[128,896]{1,0:T(8,128)(2,1)S(1)} %reshape.29.refs_0_), channel_id=1, source_target_pairs={{0,128},{1,129},{2,130},{3,131},{4,132},{5,133},{6,134},{7,135},{8... | collective-permute-start | bytes 688136 | tf_op jit(solution)/shard_map/ppermute | solution.py:55
  37.3 1.1 collective-permute-start.5
  38.4 1.6 collective-permute-start.4
  40.0 1.3 collective-permute-done.6.refs_4_
  41.3 3.3 %collective-permute-start.9 = (bf16[128,896]{1,0:T(8,128)(2,1)S(1)}, bf16[128,896]{1,0:T(8,128)(2,1)S(1)}, u32[]{:S(2)}, u32[]{:S(2)}) collective-permute-start(bf16[128,896]{1,0:T(8,128)(2,1)S(1)} %collective-permute-done.6.refs_4_), channel_id=1, source_target_pairs={{0,128},{1,129},{2,130},{3,131},{4,132},{5,133},{6,134},{7,135},{8... | collective-permute-start | bytes 688136 | tf_op jit(solution)/shard_map/ppermute | solution.py:55
  44.6 2.7 %collective-permute-start.7 = (bf16[128,896]{1,0:T(8,128)(2,1)S(1)}, bf16[128,896]{1,0:T(8,128)(2,1)S(1)}, u32[]{:S(2)}, u32[]{:S(2)}) collective-permute-start(bf16[128,896]{1,0:T(8,128)(2,1)S(1)} %collective-permute-done.3.refs_1_), channel_id=1, source_target_pairs={{0,96},{1,97},{2,98},{3,99},{4,100},{5,101},{6,102},{7,103},{8,104... | collective-permute-start | bytes 688136 | tf_op jit(solution)/shard_map/ppermute | solution.py:55
  47.3 0.7 collective-permute-done.9.refs_7_
  48.0 3.0 %collective-permute-done.8.refs_6_ = bf16[128,896]{1,0:T(8,128)(2,1)S(1)} collective-permute-done((bf16[128,896]{1,0:T(8,128)(2,1)S(1)}, bf16[128,896]{1,0:T(8,128)(2,1)S(1)}, u32[]{:S(2)}, u32[]{:S(2)}) %collective-permute-start.8) | collective-permute-done | bytes 229408 | tf_op jit(solution)/shard_map/ppermute | solution.py:55
  51.7 5.1 %inner.1.refs_0_ = bf16[128,128]{1,0:T(8,128)(2,1)} custom-call(bf16[128,896]{1,0:T(8,128)(2,1)} %copy-done.7, bf16[128,896]{1,0:T(8,128)(2,1)} %copy-done.26, bf16[128,896]{1,0:T(8,128)(2,1)} %copy-done.29, bf16[128,896]{1,0:T(8,128)(2,1)} %copy-done.28, bf16[128,896]{1,0:T(8,128)(2,1)} %copy-done.25, bf16[128,896]{1,0:T(8,128)(2,1)} %copy-done.33, ...), custom_call_target="tpu_custom_call" | custom-call | tf_op jit(solution)/shard_map/inner/pallas_call | solution.py:270
  57.0 3.6 %collective-permute-start.11 = (bf16[128,128]{1,0:T(8,128)(2,1)}, bf16[128,128]{1,0:T(8,128)(2,1)S(1)}, u32[]{:S(2)}, u32[]{:S(2)}) collective-permute-start(bf16[128,128]{1,0:T(8,128)(2,1)} %inner.1.refs_0_), channel_id=1, source_target_pairs={{0,64},{1,65},{2,66},{3,67},{4,68},{5,69},{6,70},{7,71},{8,72},{9,... | collective-permute-start | bytes 98312 | tf_op jit(solution)/shard_map/ppermute | solution.py:55
  61.1 1.4 collective-permute-done.11.refs_2_
  62.5 1.1 collective-permute-done.10.refs_1_
  64.3 3.1 %down.1 = (f32[128,896]{1,0:T(8,128)}, bf16[128,896]{1,0:T(8,128)(2,1)}) custom-call(bf16[128,128]{1,0:T(8,128)(2,1)} %inner.1.refs_0_, bf16[128,128]{1,0:T(8,128)(2,1)} %copy-done.36, bf16[128,128]{1,0:T(8,128)(2,1)} %copy-done.35, bf16[128,128]{1,0:T(8,128)(2,1)} %copy-done.34, bf16[128,1792]{1,0:T(8,128)(2,1)} %copy-done.1, bf16[128,1792]{1,0:T(8,128)(2,1)} %copy-done.11, ...), custom_call_target="tpu_custom_call" | custom-call | tf_op jit(solution)/shard_map/down/pallas_call | solution.py:299
  67.3 1.8 collective-permute-start.13
  69.1 4.8 %collective-permute-done.13 = bf16[128,896]{1,0:T(8,128)(2,1)S(1)} collective-permute-done((bf16[128,896]{1,0:T(8,128)(2,1)}, bf16[128,896]{1,0:T(8,128)(2,1)S(1)}, u32[]{:S(2)}, u32[]{:S(2)}) %collective-permute-start.13) | collective-permute-done | bytes 229408 | tf_op jit(solution)/shard_map/ppermute | solution.py:55
  73.9 1.1 add_convert_fusion
  75.0 0.7 reshape.30
  75.7 15.7 %all-to-all-start.1 = ((bf16[32,4,896]{2,1,0:T(4,128)(2,1)}), bf16[32,4,896]{2,1,0:T(4,128)(2,1)S(1)}, u32[]{:S(2)}, u32[]{:S(2)}) async-start(bf16[32,4,896]{2,1,0:T(4,128)(2,1)} %reshape.30), calls=%async_computation.1 | async-start | bytes 458752 | tf_op jit(solution)/shard_map/all_to_all | solution.py:508
  91.5 10.8 %all-to-all-done.1 = bf16[32,4,896]{2,1,0:T(4,128)(2,1)S(1)} async-done(((bf16[32,4,896]{2,1,0:T(4,128)(2,1)}), bf16[32,4,896]{2,1,0:T(4,128)(2,1)S(1)}, u32[]{:S(2)}, u32[]{:S(2)}) %all-to-all-start.1) | async-done | bytes 229408 | tf_op jit(solution)/shard_map/all_to_all | solution.py:508
  102.4 1.0 fusion
  103.5 16.8 %all_to_all.26.chunks = bf16[16,16,896]{2,1,0:T(8,128)(2,1)} all-to-all(bf16[16,16,896]{2,1,0:T(8,128)(2,1)S(1)} %broadcast_in_dim.2), channel_id=1, replica_groups=mesh['y_hi'=2,'x'=4,'y_lo'=2,'z'=8,'core'=2] {'y_hi','x','core'}, dimensions={0} | all-to-all | bytes 917504 | tf_op jit(solution)/shard_map/all_to_all | solution.py:518
  120.3 2.2 %head_norm.1 = (bf16[16,7168]{1,0:T(8,128)(2,1)}, bf16[32,7168]{1,0:T(8,128)(2,1)}, bf16[16,7168]{1,0:T(8,128)(2,1)}) custom-call(bf16[16,16,896]{2,1,0:T(8,128)(2,1)} %all_to_all.26.chunks, bf16[7168]{0:T(1024)(128)(2,1)} %gain.3), custom_call_target="tpu_custom_call" | custom-call | tf_op jit(solution)/shard_map/head_norm/pallas_call | solution.py:235
  123.0 8.3 %collective-permute-done.14.refs_1_ = bf16[32,7168]{1,0:T(8,128)(2,1)S(1)} collective-permute-done((bf16[32,7168]{1,0:T(8,128)(2,1)}, bf16[32,7168]{1,0:T(8,128)(2,1)S(1)}, u32[]{:S(2)}, u32[]{:S(2)}) %collective-permute-start.14) | collective-permute-done | bytes 458784 | tf_op jit(solution)/shard_map/ppermute | solution.py:55
  131.3 8.5 %collective-permute-done.15.refs_2_ = bf16[32,7168]{1,0:T(8,128)(2,1)S(1)} collective-permute-done((bf16[32,7168]{1,0:T(8,128)(2,1)S(1)}, bf16[32,7168]{1,0:T(8,128)(2,1)S(1)}, u32[]{:S(2)}, u32[]{:S(2)}) %collective-permute-start.15) | collective-permute-done | bytes 458784 | tf_op jit(solution)/shard_map/ppermute | solution.py:55
  139.8 6.3 %collective-permute-done.18.refs_5_ = bf16[16,7168]{1,0:T(8,128)(2,1)S(1)} collective-permute-done((bf16[16,7168]{1,0:T(8,128)(2,1)}, bf16[16,7168]{1,0:T(8,128)(2,1)S(1)}, u32[]{:S(2)}, u32[]{:S(2)}) %collective-permute-start.18) | collective-permute-done | bytes 229408 | tf_op jit(solution)/shard_map/ppermute | solution.py:55
  146.1 3.6 %collective-permute-start.27 = (bf16[16,7168]{1,0:T(8,128)(2,1)S(1)}, bf16[16,7168]{1,0:T(8,128)(2,1)}, u32[]{:S(2)}, u32[]{:S(2)}) collective-permute-start(bf16[16,7168]{1,0:T(8,128)(2,1)S(1)} %collective-permute-done.18.refs_5_), channel_id=1, source_target_pairs={{0,1},{1,0},{2,3},{3,2},{4,5},{5,4},{6,7},{7,6},{8,9},{9,8},{10,11... | collective-permute-start | bytes 688136 | tf_op jit(solution)/shard_map/ppermute | solution.py:55
  149.7 1.7 collective-permute-start.28
  152.0 1.3 collective-permute-start.24
  153.6 4.6 %collective-permute-done.20.refs_7_ = bf16[32,7168]{1,0:T(8,128)(2,1)S(1)} collective-permute-done((bf16[32,7168]{1,0:T(8,128)(2,1)S(1)}, bf16[32,7168]{1,0:T(8,128)(2,1)S(1)}, u32[]{:S(2)}, u32[]{:S(2)}) %collective-permute-start.20) | collective-permute-done | bytes 458784 | tf_op jit(solution)/shard_map/ppermute | solution.py:55
  158.7 0.7 collective-permute-done.17.refs_4_
  159.4 3.7 %collective-permute-done.21.refs_8_ = bf16[32,7168]{1,0:T(8,128)(2,1)S(1)} collective-permute-done((bf16[32,7168]{1,0:T(8,128)(2,1)S(1)}, bf16[32,7168]{1,0:T(8,128)(2,1)S(1)}, u32[]{:S(2)}, u32[]{:S(2)}) %collective-permute-start.21) | collective-permute-done | bytes 458784 | tf_op jit(solution)/shard_map/ppermute | solution.py:55
  163.9 1.7 collective-permute-done.22.refs_9_
  166.1 1.1 collective-permute-done.31.refs_18_
  168.6 8.6 %logits.1 = (f32[256,512]{1,0:T(8,128)}, f32[16,12,128]{2,1,0:T(8,128)}, bf16[512,7168]{1,0:T(8,128)(2,1)}) custom-call(bf16[32,7168]{1,0:T(8,128)(2,1)} %get-tuple-element.38.refs_0_, bf16[32,7168]{1,0:T(8,128)(2,1)} %copy-done.8, bf16[32,7168]{1,0:T(8,128)(2,1)} %copy-done.9, bf16[32,7168]{1,0:T(8,128)(2,1)} %copy-done.6, bf16[16,7168]{1,0:T(8,128)(2,1)} %copy-done.23, ...), custom_call_target="tpu_custom_call" | custom-call | tf_op jit(solution)/shard_map/logits/pallas_call | solution.py:372
  177.2 12.0 %all_to_all.27.parts = f32[16,12,128]{2,1,0:T(8,128)} all-to-all(f32[16,12,128]{2,1,0:T(8,128)} %get-tuple-element.41), channel_id=1, replica_groups=mesh['y_hi'=2,'x'=4,'y_lo'=2,'z'=8,'core'=2] {'y_hi','x','core'}, dimensions={0} | all-to-all | bytes 196608 | tf_op jit(solution)/shard_map/all_to_all | solution.py:529
  189.3 1.6 join.1
  190.9 12.1 %all_to_all.28.parts = f32[16,12,128]{2,1,0:T(8,128)} all-to-all(f32[16,12,128]{2,1,0:T(8,128)} %join.1), channel_id=1, replica_groups=mesh['y_hi'=2,'x'=4,'y_lo'=2,'z'=8,'core'=2] {'y_lo','z'}, dimensions={0} | all-to-all | bytes 196608 | tf_op jit(solution)/shard_map/all_to_all | solution.py:531
  203.0 7.0 %head_grad.1 = (f32[4,128]{1,0:T(4,128)}, bf16[256,7168]{1,0:T(8,128)(2,1)}) custom-call(bf16[512,7168]{1,0:T(8,128)(2,1)} %get-tuple-element.40.gathered, f32[16,12,128]{2,1,0:T(8,128)} %all_to_all.28.parts, f32[256,512]{1,0:T(8,128)} %get-tuple-element.42.logits, s32[1,512]{1,0:T(1,128)} %bitcast.16, f32[1,512]{1,0:T(1,128)} %bitcast.17), custom_call_target="tpu_custom_call" | custom-call | tf_op jit(solution)/shard_map/head_grad/pallas_call | solution.py:463
  (111 shorter events, 8.5 us)
Async XLA Ops:
  6.6 26.3 %collective-permute-start = (bf16[128,1792]{1,0:T(8,128)(2,1)S(1)}, bf16[128,1792]{1,0:T(8,128)(2,1)S(1)}, u32[]{:S(2)}, u32[]{:S(2)}) collective-permute-start(bf16[128,1792]{1,0:T(8,128)(2,1)S(1)} %get-tuple-element.27), channel_id=1, source_target_pairs={{0,96},{1,97},{2,98},{3,99},{4,100},{5,101},{6,102},{7,103},{8,104... | collective-permute-start | bytes 1376264 | tf_op jit(solution)/shard_map/ppermute | solution.py:55
  9.9 23.0 %collective-permute-start.1 = (bf16[128,1792]{1,0:T(8,128)(2,1)S(1)}, bf16[128,1792]{1,0:T(8,128)(2,1)S(1)}, u32[]{:S(2)}, u32[]{:S(2)}) collective-permute-start(bf16[128,1792]{1,0:T(8,128)(2,1)S(1)} %get-tuple-element.28), channel_id=1, source_target_pairs={{0,64},{1,65},{2,66},{3,67},{4,68},{5,69},{6,70},{7,71},{8,72},{9,... | collective-permute-start | bytes 1376264 | tf_op jit(solution)/shard_map/ppermute | solution.py:55
  10.4 23.3 %collective-permute-start.2 = (bf16[128,1792]{1,0:T(8,128)(2,1)S(1)}, bf16[128,1792]{1,0:T(8,128)(2,1)S(1)}, u32[]{:S(2)}, u32[]{:S(2)}) collective-permute-start(bf16[128,1792]{1,0:T(8,128)(2,1)S(1)} %get-tuple-element.29), channel_id=1, source_target_pairs={{0,32},{1,33},{2,34},{3,35},{4,36},{5,37},{6,38},{7,39},{8,40},{9,... | collective-permute-start | bytes 1376264 | tf_op jit(solution)/shard_map/ppermute | solution.py:55
  32.9 30.7 %copy-start.11 = (bf16[128,1792]{1,0:T(8,128)(2,1)}, bf16[128,1792]{1,0:T(8,128)(2,1)S(1)}, u32[]{:S(2)}) copy-start(bf16[128,1792]{1,0:T(8,128)(2,1)S(1)} %collective-permute-done.refs_5_) | copy-start | bytes 1376260
  32.9 30.7 %copy-start.12 = (bf16[128,1792]{1,0:T(8,128)(2,1)}, bf16[128,1792]{1,0:T(8,128)(2,1)S(1)}, u32[]{:S(2)}) copy-start(bf16[128,1792]{1,0:T(8,128)(2,1)S(1)} %collective-permute-done.1.refs_6_) | copy-start | bytes 1376260
  33.7 30.0 %copy-start.13 = (bf16[128,1792]{1,0:T(8,128)(2,1)}, bf16[128,1792]{1,0:T(8,128)(2,1)S(1)}, u32[]{:S(2)}) copy-start(bf16[128,1792]{1,0:T(8,128)(2,1)S(1)} %collective-permute-done.2.refs_7_) | copy-start | bytes 1376260
  33.7 17.2 %copy-start.7 = (bf16[128,896]{1,0:T(8,128)(2,1)}, bf16[128,896]{1,0:T(8,128)(2,1)S(1)}, u32[]{:S(2)}) copy-start(bf16[128,896]{1,0:T(8,128)(2,1)S(1)} %reshape.29.refs_0_) | copy-start | bytes 688132
  33.7 7.6 %collective-permute-start.6 = (bf16[128,896]{1,0:T(8,128)(2,1)S(1)}, bf16[128,896]{1,0:T(8,128)(2,1)S(1)}, u32[]{:S(2)}, u32[]{:S(2)}) collective-permute-start(bf16[128,896]{1,0:T(8,128)(2,1)S(1)} %reshape.29.refs_0_), channel_id=1, source_target_pairs={{0,64},{1,65},{2,66},{3,67},{4,68},{5,69},{6,70},{7,71},{8,72},{9,... | collective-permute-start | bytes 688136 | tf_op jit(solution)/shard_map/ppermute | solution.py:55
  34.7 9.9 %collective-permute-start.3 = (bf16[128,896]{1,0:T(8,128)(2,1)S(1)}, bf16[128,896]{1,0:T(8,128)(2,1)S(1)}, u32[]{:S(2)}, u32[]{:S(2)}) collective-permute-start(bf16[128,896]{1,0:T(8,128)(2,1)S(1)} %reshape.29.refs_0_), channel_id=1, source_target_pairs={{0,128},{1,129},{2,130},{3,131},{4,132},{5,133},{6,134},{7,135},{8... | collective-permute-start | bytes 688136 | tf_op jit(solution)/shard_map/ppermute | solution.py:55
  37.3 10.0 %collective-permute-start.5 = (bf16[128,896]{1,0:T(8,128)(2,1)S(1)}, bf16[128,896]{1,0:T(8,128)(2,1)S(1)}, u32[]{:S(2)}, u32[]{:S(2)}) collective-permute-start(bf16[128,896]{1,0:T(8,128)(2,1)S(1)} %reshape.29.refs_0_), channel_id=1, source_target_pairs={{0,32},{1,33},{2,34},{3,35},{4,36},{5,37},{6,38},{7,39},{8,40},{9,... | collective-permute-start | bytes 688136 | tf_op jit(solution)/shard_map/ppermute | solution.py:55
  38.4 8.9 %collective-permute-start.4 = (bf16[128,896]{1,0:T(8,128)(2,1)S(1)}, bf16[128,896]{1,0:T(8,128)(2,1)S(1)}, u32[]{:S(2)}, u32[]{:S(2)}) collective-permute-start(bf16[128,896]{1,0:T(8,128)(2,1)S(1)} %reshape.29.refs_0_), channel_id=1, source_target_pairs={{0,96},{1,97},{2,98},{3,99},{4,100},{5,101},{6,102},{7,103},{8,104... | collective-permute-start | bytes 688136 | tf_op jit(solution)/shard_map/ppermute | solution.py:55
  41.3 9.7 %copy-start.25 = (bf16[128,896]{1,0:T(8,128)(2,1)}, bf16[128,896]{1,0:T(8,128)(2,1)S(1)}, u32[]{:S(2)}) copy-start(bf16[128,896]{1,0:T(8,128)(2,1)S(1)} %collective-permute-done.6.refs_4_) | copy-start | bytes 688132
  41.3 6.7 %collective-permute-start.9 = (bf16[128,896]{1,0:T(8,128)(2,1)S(1)}, bf16[128,896]{1,0:T(8,128)(2,1)S(1)}, u32[]{:S(2)}, u32[]{:S(2)}) collective-permute-start(bf16[128,896]{1,0:T(8,128)(2,1)S(1)} %collective-permute-done.6.refs_4_), channel_id=1, source_target_pairs={{0,128},{1,129},{2,130},{3,131},{4,132},{5,133},{6,134},{7,135},{8... | collective-permute-start | bytes 688136 | tf_op jit(solution)/shard_map/ppermute | solution.py:55
  44.6 6.4 %copy-start.26 = (bf16[128,896]{1,0:T(8,128)(2,1)}, bf16[128,896]{1,0:T(8,128)(2,1)S(1)}, u32[]{:S(2)}) copy-start(bf16[128,896]{1,0:T(8,128)(2,1)S(1)} %collective-permute-done.3.refs_1_) | copy-start | bytes 688132
  44.6 6.4 %collective-permute-start.8 = (bf16[128,896]{1,0:T(8,128)(2,1)S(1)}, bf16[128,896]{1,0:T(8,128)(2,1)S(1)}, u32[]{:S(2)}, u32[]{:S(2)}) collective-permute-start(bf16[128,896]{1,0:T(8,128)(2,1)S(1)} %collective-permute-done.3.refs_1_), channel_id=1, source_target_pairs={{0,32},{1,33},{2,34},{3,35},{4,36},{5,37},{6,38},{7,39},{8,40},{9,... | collective-permute-start | bytes 688136 | tf_op jit(solution)/shard_map/ppermute | solution.py:55
  44.6 6.4 %collective-permute-start.7 = (bf16[128,896]{1,0:T(8,128)(2,1)S(1)}, bf16[128,896]{1,0:T(8,128)(2,1)S(1)}, u32[]{:S(2)}, u32[]{:S(2)}) collective-permute-start(bf16[128,896]{1,0:T(8,128)(2,1)S(1)} %collective-permute-done.3.refs_1_), channel_id=1, source_target_pairs={{0,96},{1,97},{2,98},{3,99},{4,100},{5,101},{6,102},{7,103},{8,104... | collective-permute-start | bytes 688136 | tf_op jit(solution)/shard_map/ppermute | solution.py:55
  56.9 4.3 %collective-permute-start.12 = (bf16[128,128]{1,0:T(8,128)(2,1)}, bf16[128,128]{1,0:T(8,128)(2,1)S(1)}, u32[]{:S(2)}, u32[]{:S(2)}) collective-permute-start(bf16[128,128]{1,0:T(8,128)(2,1)} %inner.1.refs_0_), channel_id=1, source_target_pairs={{0,32},{1,33},{2,34},{3,35},{4,36},{5,37},{6,38},{7,39},{8,40},{9,... | collective-permute-start | bytes 98312 | tf_op jit(solution)/shard_map/ppermute | solution.py:55
  57.0 5.5 %collective-permute-start.11 = (bf16[128,128]{1,0:T(8,128)(2,1)}, bf16[128,128]{1,0:T(8,128)(2,1)S(1)}, u32[]{:S(2)}, u32[]{:S(2)}) collective-permute-start(bf16[128,128]{1,0:T(8,128)(2,1)} %inner.1.refs_0_), channel_id=1, source_target_pairs={{0,64},{1,65},{2,66},{3,67},{4,68},{5,69},{6,70},{7,71},{8,72},{9,... | collective-permute-start | bytes 98312 | tf_op jit(solution)/shard_map/ppermute | solution.py:55
  60.7 3.0 %collective-permute-start.10 = (bf16[128,128]{1,0:T(8,128)(2,1)}, bf16[128,128]{1,0:T(8,128)(2,1)S(1)}, u32[]{:S(2)}, u32[]{:S(2)}) collective-permute-start(bf16[128,128]{1,0:T(8,128)(2,1)} %inner.1.refs_0_), channel_id=1, source_target_pairs={{0,96},{1,97},{2,98},{3,99},{4,100},{5,101},{6,102},{7,103},{8,104... | collective-permute-start | bytes 98312 | tf_op jit(solution)/shard_map/ppermute | solution.py:55
  67.3 6.6 %collective-permute-start.13 = (bf16[128,896]{1,0:T(8,128)(2,1)}, bf16[128,896]{1,0:T(8,128)(2,1)S(1)}, u32[]{:S(2)}, u32[]{:S(2)}) collective-permute-start(bf16[128,896]{1,0:T(8,128)(2,1)} %get-tuple-element.36), channel_id=1, source_target_pairs={{0,128},{1,129},{2,130},{3,131},{4,132},{5,133},{6,134},{7,135},{8... | collective-permute-start | bytes 688136 | tf_op jit(solution)/shard_map/ppermute | solution.py:55
  75.7 26.6 %all-to-all-start.1 = ((bf16[32,4,896]{2,1,0:T(4,128)(2,1)}), bf16[32,4,896]{2,1,0:T(4,128)(2,1)S(1)}, u32[]{:S(2)}, u32[]{:S(2)}) async-start(bf16[32,4,896]{2,1,0:T(4,128)(2,1)} %reshape.30), calls=%async_computation.1 | async-start | bytes 458752 | tf_op jit(solution)/shard_map/all_to_all | solution.py:508
  122.5 8.8 %collective-permute-start.14 = (bf16[32,7168]{1,0:T(8,128)(2,1)}, bf16[32,7168]{1,0:T(8,128)(2,1)S(1)}, u32[]{:S(2)}, u32[]{:S(2)}) collective-permute-start(bf16[32,7168]{1,0:T(8,128)(2,1)} %get-tuple-element.38.refs_0_), channel_id=1, source_target_pairs={{0,14},{1,3},{2,0},{3,5},{4,2},{5,7},{6,4},{7,9},{8,6},{9,11},{10,... | collective-permute-start | bytes 1376264 | tf_op jit(solution)/shard_map/ppermute | solution.py:55
  131.3 36.6 %copy-start.8 = (bf16[32,7168]{1,0:T(8,128)(2,1)}, bf16[32,7168]{1,0:T(8,128)(2,1)S(1)}, u32[]{:S(2)}) copy-start(bf16[32,7168]{1,0:T(8,128)(2,1)S(1)} %collective-permute-done.14.refs_1_) | copy-start | bytes 1376260
  131.3 8.5 %collective-permute-start.15 = (bf16[32,7168]{1,0:T(8,128)(2,1)S(1)}, bf16[32,7168]{1,0:T(8,128)(2,1)S(1)}, u32[]{:S(2)}, u32[]{:S(2)}) collective-permute-start(bf16[32,7168]{1,0:T(8,128)(2,1)S(1)} %collective-permute-done.14.refs_1_), channel_id=1, source_target_pairs={{0,14},{1,3},{2,0},{3,5},{4,2},{5,7},{6,4},{7,9},{8,6},{9,11},{10,... | collective-permute-start | bytes 1376264 | tf_op jit(solution)/shard_map/ppermute | solution.py:55
  131.3 18.4 %collective-permute-start.19 = (bf16[32,7168]{1,0:T(8,128)(2,1)S(1)}, bf16[32,7168]{1,0:T(8,128)(2,1)S(1)}, u32[]{:S(2)}, u32[]{:S(2)}) collective-permute-start(bf16[32,7168]{1,0:T(8,128)(2,1)S(1)} %collective-permute-done.14.refs_1_), channel_id=1, source_target_pairs={{0,144},{1,17},{2,146},{3,19},{4,148},{5,21},{6,150},{7,23},{8,152... | collective-permute-start | bytes 1376264 | tf_op jit(solution)/shard_map/ppermute | solution.py:55
  139.8 28.0 %copy-start.9 = (bf16[32,7168]{1,0:T(8,128)(2,1)}, bf16[32,7168]{1,0:T(8,128)(2,1)S(1)}, u32[]{:S(2)}) copy-start(bf16[32,7168]{1,0:T(8,128)(2,1)S(1)} %collective-permute-done.15.refs_2_) | copy-start | bytes 1376260
  139.8 11.6 %collective-permute-start.16 = (bf16[32,7168]{1,0:T(8,128)(2,1)S(1)}, bf16[32,7168]{1,0:T(8,128)(2,1)S(1)}, u32[]{:S(2)}, u32[]{:S(2)}) collective-permute-start(bf16[32,7168]{1,0:T(8,128)(2,1)S(1)} %collective-permute-done.15.refs_2_), channel_id=1, source_target_pairs={{0,14},{1,3},{2,0},{3,5},{4,2},{5,7},{6,4},{7,9},{8,6},{9,11},{10,... | collective-permute-start | bytes 1376264 | tf_op jit(solution)/shard_map/ppermute | solution.py:55
  139.8 6.3 %collective-permute-start.18 = (bf16[16,7168]{1,0:T(8,128)(2,1)}, bf16[16,7168]{1,0:T(8,128)(2,1)S(1)}, u32[]{:S(2)}, u32[]{:S(2)}) collective-permute-start(bf16[16,7168]{1,0:T(8,128)(2,1)} %get-tuple-element.39), channel_id=1, source_target_pairs={{0,144},{1,17},{2,146},{3,19},{4,148},{5,21},{6,150},{7,23},{8,152... | collective-permute-start | bytes 688136 | tf_op jit(solution)/shard_map/ppermute | solution.py:55
  146.1 21.7 %copy-start.22 = (bf16[16,7168]{1,0:T(8,128)(2,1)}, bf16[16,7168]{1,0:T(8,128)(2,1)S(1)}, u32[]{:S(2)}) copy-start(bf16[16,7168]{1,0:T(8,128)(2,1)S(1)} %collective-permute-done.18.refs_5_) | copy-start | bytes 688132
  146.1 5.9 %collective-permute-start.27 = (bf16[16,7168]{1,0:T(8,128)(2,1)S(1)}, bf16[16,7168]{1,0:T(8,128)(2,1)}, u32[]{:S(2)}, u32[]{:S(2)}) collective-permute-start(bf16[16,7168]{1,0:T(8,128)(2,1)S(1)} %collective-permute-done.18.refs_5_), channel_id=1, source_target_pairs={{0,1},{1,0},{2,3},{3,2},{4,5},{5,4},{6,7},{7,6},{8,9},{9,8},{10,11... | collective-permute-start | bytes 688136 | tf_op jit(solution)/shard_map/ppermute | solution.py:55
  149.7 3.6 %collective-permute-start.23 = (bf16[32,7168]{1,0:T(8,128)(2,1)S(1)}, bf16[32,7168]{1,0:T(8,128)(2,1)S(1)}, u32[]{:S(2)}, u32[]{:S(2)}) collective-permute-start(bf16[32,7168]{1,0:T(8,128)(2,1)S(1)} %collective-permute-done.14.refs_1_), channel_id=1, source_target_pairs={{0,1},{1,0},{2,3},{3,2},{4,5},{5,4},{6,7},{7,6},{8,9},{9,8},{10,11... | collective-permute-start | bytes 1376264 | tf_op jit(solution)/shard_map/ppermute | solution.py:55
  149.7 8.5 %collective-permute-start.20 = (bf16[32,7168]{1,0:T(8,128)(2,1)S(1)}, bf16[32,7168]{1,0:T(8,128)(2,1)S(1)}, u32[]{:S(2)}, u32[]{:S(2)}) collective-permute-start(bf16[32,7168]{1,0:T(8,128)(2,1)S(1)} %collective-permute-done.15.refs_2_), channel_id=1, source_target_pairs={{0,144},{1,17},{2,146},{3,19},{4,148},{5,21},{6,150},{7,23},{8,152... | collective-permute-start | bytes 1376264 | tf_op jit(solution)/shard_map/ppermute | solution.py:55
  149.7 18.2 %copy-start.10 = (bf16[32,7168]{1,0:T(8,128)(2,1)}, bf16[32,7168]{1,0:T(8,128)(2,1)S(1)}, u32[]{:S(2)}) copy-start(bf16[32,7168]{1,0:T(8,128)(2,1)S(1)} %collective-permute-done.19.refs_6_) | copy-start | bytes 1376260
  149.7 3.6 %collective-permute-start.28 = (bf16[32,7168]{1,0:T(8,128)(2,1)S(1)}, bf16[32,7168]{1,0:T(8,128)(2,1)S(1)}, u32[]{:S(2)}, u32[]{:S(2)}) collective-permute-start(bf16[32,7168]{1,0:T(8,128)(2,1)S(1)} %collective-permute-done.19.refs_6_), channel_id=1, source_target_pairs={{0,1},{1,0},{2,3},{3,2},{4,5},{5,4},{6,7},{7,6},{8,9},{9,8},{10,11... | collective-permute-start | bytes 1376264 | tf_op jit(solution)/shard_map/ppermute | solution.py:55
  151.4 16.5 %copy-start.6 = (bf16[32,7168]{1,0:T(8,128)(2,1)}, bf16[32,7168]{1,0:T(8,128)(2,1)S(1)}, u32[]{:S(2)}) copy-start(bf16[32,7168]{1,0:T(8,128)(2,1)S(1)} %collective-permute-done.16.refs_3_) | copy-start | bytes 1376260
  151.4 11.7 %collective-permute-start.21 = (bf16[32,7168]{1,0:T(8,128)(2,1)S(1)}, bf16[32,7168]{1,0:T(8,128)(2,1)S(1)}, u32[]{:S(2)}, u32[]{:S(2)}) collective-permute-start(bf16[32,7168]{1,0:T(8,128)(2,1)S(1)} %collective-permute-done.16.refs_3_), channel_id=1, source_target_pairs={{0,144},{1,17},{2,146},{3,19},{4,148},{5,21},{6,150},{7,23},{8,152... | collective-permute-start | bytes 1376264 | tf_op jit(solution)/shard_map/ppermute | solution.py:55
  152.0 11.6 %collective-permute-start.24 = (bf16[32,7168]{1,0:T(8,128)(2,1)S(1)}, bf16[32,7168]{1,0:T(8,128)(2,1)S(1)}, u32[]{:S(2)}, u32[]{:S(2)}) collective-permute-start(bf16[32,7168]{1,0:T(8,128)(2,1)S(1)} %collective-permute-done.15.refs_2_), channel_id=1, source_target_pairs={{0,1},{1,0},{2,3},{3,2},{4,5},{5,4},{6,7},{7,6},{8,9},{9,8},{10,11... | collective-permute-start | bytes 1376264 | tf_op jit(solution)/shard_map/ppermute | solution.py:55
  153.3 14.6 %copy-start.14 = (bf16[32,7168]{1,0:T(8,128)(2,1)}, bf16[32,7168]{1,0:T(8,128)(2,1)S(1)}, u32[]{:S(2)}) copy-start(bf16[32,7168]{1,0:T(8,128)(2,1)S(1)} %collective-permute-done.23.refs_10_) | copy-start | bytes 1376260
  153.3 6.1 %collective-permute-start.17 = (bf16[16,7168]{1,0:T(8,128)(2,1)S(1)}, bf16[16,7168]{1,0:T(8,128)(2,1)S(1)}, u32[]{:S(2)}, u32[]{:S(2)}) collective-permute-start(bf16[16,7168]{1,0:T(8,128)(2,1)S(1)} %constant_dynamic-slice_fusion), channel_id=1, source_target_pairs={{0,14},{1,3},{2,0},{3,5},{4,2},{5,7},{6,4},{7,9},{8,6},{9,11},{10,... | collective-permute-start | bytes 688136 | tf_op jit(solution)/shard_map/ppermute | solution.py:55
  153.3 14.6 %copy-start.16 = (bf16[32,7168]{1,0:T(8,128)(2,1)}, bf16[32,7168]{1,0:T(8,128)(2,1)S(1)}, u32[]{:S(2)}) copy-start(bf16[32,7168]{1,0:T(8,128)(2,1)S(1)} %collective-permute-done.28.refs_15_) | copy-start | bytes 1376260
  153.3 12.8 %collective-permute-start.25 = (bf16[32,7168]{1,0:T(8,128)(2,1)S(1)}, bf16[32,7168]{1,0:T(8,128)(2,1)S(1)}, u32[]{:S(2)}, u32[]{:S(2)}) collective-permute-start(bf16[32,7168]{1,0:T(8,128)(2,1)S(1)} %collective-permute-done.16.refs_3_), channel_id=1, source_target_pairs={{0,1},{1,0},{2,3},{3,2},{4,5},{5,4},{6,7},{7,6},{8,9},{9,8},{10,11... | collective-permute-start | bytes 1376264 | tf_op jit(solution)/shard_map/ppermute | solution.py:55
  158.2 9.7 %copy-start.15 = (bf16[32,7168]{1,0:T(8,128)(2,1)}, bf16[32,7168]{1,0:T(8,128)(2,1)S(1)}, u32[]{:S(2)}) copy-start(bf16[32,7168]{1,0:T(8,128)(2,1)S(1)} %collective-permute-done.20.refs_7_) | copy-start | bytes 1376260
  158.2 7.8 %collective-permute-start.29 = (bf16[32,7168]{1,0:T(8,128)(2,1)S(1)}, bf16[32,7168]{1,0:T(8,128)(2,1)S(1)}, u32[]{:S(2)}, u32[]{:S(2)}) collective-permute-start(bf16[32,7168]{1,0:T(8,128)(2,1)S(1)} %collective-permute-done.20.refs_7_), channel_id=1, source_target_pairs={{0,1},{1,0},{2,3},{3,2},{4,5},{5,4},{6,7},{7,6},{8,9},{9,8},{10,11... | collective-permute-start | bytes 1376264 | tf_op jit(solution)/shard_map/ppermute | solution.py:55
  159.3 7.8 %copy-start.23 = (bf16[16,7168]{1,0:T(8,128)(2,1)}, bf16[16,7168]{1,0:T(8,128)(2,1)S(1)}, u32[]{:S(2)}) copy-start(bf16[16,7168]{1,0:T(8,128)(2,1)S(1)} %collective-permute-done.17.refs_4_) | copy-start | bytes 688132
  159.4 6.2 %collective-permute-start.22 = (bf16[16,7168]{1,0:T(8,128)(2,1)S(1)}, bf16[16,7168]{1,0:T(8,128)(2,1)S(1)}, u32[]{:S(2)}, u32[]{:S(2)}) collective-permute-start(bf16[16,7168]{1,0:T(8,128)(2,1)S(1)} %collective-permute-done.17.refs_4_), channel_id=1, source_target_pairs={{0,144},{1,17},{2,146},{3,19},{4,148},{5,21},{6,150},{7,23},{8,152... | collective-permute-start | bytes 688136 | tf_op jit(solution)/shard_map/ppermute | solution.py:55
  163.1 4.0 %collective-permute-start.30 = (bf16[32,7168]{1,0:T(8,128)(2,1)S(1)}, bf16[32,7168]{1,0:T(8,128)(2,1)S(1)}, u32[]{:S(2)}, u32[]{:S(2)}) collective-permute-start(bf16[32,7168]{1,0:T(8,128)(2,1)S(1)} %collective-permute-done.21.refs_8_), channel_id=1, source_target_pairs={{0,1},{1,0},{2,3},{3,2},{4,5},{5,4},{6,7},{7,6},{8,9},{9,8},{10,11... | collective-permute-start | bytes 1376264 | tf_op jit(solution)/shard_map/ppermute | solution.py:55
  163.6 2.5 %collective-permute-start.26 = (bf16[16,7168]{1,0:T(8,128)(2,1)S(1)}, bf16[16,7168]{1,0:T(8,128)(2,1)S(1)}, u32[]{:S(2)}, u32[]{:S(2)}) collective-permute-start(bf16[16,7168]{1,0:T(8,128)(2,1)S(1)} %collective-permute-done.17.refs_4_), channel_id=1, source_target_pairs={{0,1},{1,0},{2,3},{3,2},{4,5},{5,4},{6,7},{7,6},{8,9},{9,8},{10,11... | collective-permute-start | bytes 688136 | tf_op jit(solution)/shard_map/ppermute | solution.py:55
  165.6 1.6 collective-permute-start.31
  (22 other events, 39.3 us)
